TPU v7x, 128 devices: a whole 4x4x4 slice. The times are simulated.
128 devices in a mesh: dp: 4 (over y_hi, core), ctx: 32 (over y_lo, z, x).
Axes of the slice: x: 4, y: 4 (y_hi: 2, y_lo: 2; y = y_hi * 2 + y_lo), z: 4, core: 2. Of those that a mesh axis runs over, the one named last changes fastest.
Arguments:
- trunk_input: bfloat16 [4, 8192, 768], P('dp', 'ctx'), may hold values from -6 to 6
- tokens: int32 [4, 8192], P('dp', 'ctx'), may hold values from 0 to 3
- token_table: float32 [4, 768], replicated, may hold values from -3 to 3
- conv_weight: bfloat16 [2, 3, 768, 384], replicated, may hold values from -0.125 to 0.125
- out_weight: bfloat16 [2, 384, 768], replicated, may hold values from -0.3125 to 0.3125
- norm_gain: float32 [2, 768], replicated, may hold values from 0.1 to 1.9
- mid_gain: float32 [2, 384], replicated, may hold values from 0.1 to 1.9
- strand_perm: int32 [768], replicated, may hold values from 0 to 767, each once
- dilation: int32 [2], replicated, may hold values from 1 to 64, as said below
- out_cotangent: bfloat16 [4, 8192, 768], P('dp', 'ctx'), may hold values from -6 to 6
Outputs:
- block_output: bfloat16 [4, 8192, 768], P('dp', 'ctx')
- trunk_grad: bfloat16 [4, 8192, 768], P('dp', 'ctx')
- table_grad: float32 [4, 768], replicated
- conv_grad: float32 [2, 3, 768, 384], replicated
- out_weight_grad: float32 [2, 384, 768], replicated
- norm_gain_grad: float32 [2, 768], replicated
- mid_gain_grad: float32 [2, 384], replicated
Inputs may be any that keep to these rules, and one draw needn't show every extreme that they name: Each block's dilation lies in 1 .. 64, and some block has exactly 64. `strand_perm`: each channel index appears once.
All inputs are finite; a program needn't handle non-finite values.
Results may differ from a plain program's by a relative error of at most 0.014.
Values may be sent and summed in bfloat16 or wider, within the bound.
A program may use at most 128 MiB of HBM per device.

v0:
```python
import jax
import jax.numpy as jnp
from jax import lax
from jax.sharding import PartitionSpec as P

LAYERS = 2
DMAX = 64


epsilon = 1e-05
precise = lax.Precision.HIGHEST


def with_halo(block, sides, width):
    for axis, dim in sides:
        count = lax.axis_size(axis)
        forward = [(i, i + 1) for i in range(count - 1)]
        backward = [(target, source) for source, target in forward]
        low = lax.ppermute(
            lax.slice_in_dim(block, block.shape[dim] - width, None, axis=dim), axis, forward
        )
        high = lax.ppermute(lax.slice_in_dim(block, 0, width, axis=dim), axis, backward)
        block = jnp.concatenate([low, block, high], axis=dim)
    return block


def swapped(value, axis, apart):
    return lax.ppermute(value, axis, [(i, i ^ 1 << apart) for i in range(lax.axis_size(axis))])


def normed_act(values, scaling):
    centre = jnp.mean(values, axis=-1, keepdims=True)
    shifted = values - centre
    spread = jnp.mean(shifted * shifted, axis=-1, keepdims=True)
    return jax.nn.gelu(shifted * lax.rsqrt(spread + epsilon) * scaling, approximate=False)


def matmul(left, right):
    flat = left.reshape(-1, left.shape[-1])
    product = jnp.dot(flat, right, preferred_element_type=jnp.float32)
    return product.reshape(left.shape[:-1] + (right.shape[-1],))


def matmul_t(left, right):
    flat = left.reshape(-1, left.shape[-1])
    product = lax.dot_general(
        flat, right, (((1,), (1,)), ((), ())), preferred_element_type=jnp.float32
    )
    return product.reshape(left.shape[:-1] + (right.shape[0],))


def outer_sum(left, right):
    flat_left = left.reshape(-1, left.shape[-1])
    flat_right = right.reshape(-1, right.shape[-1])
    return lax.dot_general(
        flat_left, flat_right, (((0,), (0,)), ((), ())), preferred_element_type=jnp.float32
    )


def settle(values):
    return lax.optimization_barrier(values.astype(jnp.bfloat16)).astype(jnp.float32)


def three_taps(padded, dilate, length):
    offset_low = DMAX - dilate
    offset_high = DMAX + dilate
    before = lax.dynamic_slice_in_dim(padded, offset_low, length, 1)
    centre = padded[:, DMAX : DMAX + length]
    behind = lax.dynamic_slice_in_dim(padded, offset_high, length, 1)
    return (before, centre, behind)


def front(hidden, scaling):
    return normed_act(hidden.astype(jnp.float32), scaling).astype(jnp.bfloat16)


def halo_pair(front_pair):
    return with_halo(front_pair, (("ctx", 2),), DMAX)


def middle(padded, conv_w, dilate, length):
    before, centre, behind = three_taps(padded, dilate, length)
    return matmul(before, conv_w[0]) + matmul(centre, conv_w[1]) + matmul(behind, conv_w[2])


def finish(mid_values, out_w, mid_scale):
    squashed = normed_act(mid_values, mid_scale).astype(jnp.bfloat16)
    return matmul(squashed, out_w)


def grad_back(mid_values, cotangent, out_w, mid_scale):
    squashed, act_vjp = jax.vjp(normed_act, mid_values, mid_scale)
    rounded = squashed.astype(jnp.bfloat16)
    d_out_w = outer_sum(rounded, cotangent)
    d_squashed = matmul_t(cotangent, out_w)
    d_mid, d_mid_scale = act_vjp(d_squashed)
    return (d_mid.astype(jnp.bfloat16), d_out_w, d_mid_scale)


def grad_front(padded_u, padded_dm, conv_w, dilate, length, hidden, scaling):
    u_before, u_centre, u_behind = three_taps(padded_u, dilate, length)
    d_before, d_centre, d_behind = three_taps(padded_dm, dilate, length)
    d_conv = jnp.stack(
        [
            outer_sum(u_before, d_centre),
            outer_sum(u_centre, d_centre),
            outer_sum(u_behind, d_centre),
        ]
    )
    d_front = (
        matmul_t(d_behind, conv_w[0])
        + matmul_t(d_centre, conv_w[1])
        + matmul_t(d_before, conv_w[2])
    )
    primal_out, front_vjp = jax.vjp(normed_act, hidden.astype(jnp.float32), scaling)
    d_hidden, d_scaling = front_vjp(d_front)
    return (d_hidden, d_conv, d_scaling)


def mirror_bins(values):
    flipped = values[:, ::-1]
    bit_count = lax.axis_size("ctx").bit_length() - 1
    for bit_index in range(bit_count):
        flipped = swapped(flipped, "ctx", bit_index)
    return flipped


def reverse_strand(values, strand_perm):
    return jnp.take(mirror_bins(values), strand_perm, axis=2)


def restore_strand(values, inverse):
    return jnp.take(mirror_bins(values), inverse, axis=2)


def embed(one_hot, token_table):
    flat = one_hot.reshape(-1, 4)
    product = jnp.dot(flat, token_table, precision=precise, preferred_element_type=jnp.float32)
    return product.reshape(one_hot.shape[:-1] + (token_table.shape[-1],))


def table_term(one_hot, grad):
    flat_hot = one_hot.reshape(-1, 4)
    flat_grad = grad.reshape(-1, grad.shape[-1]).astype(jnp.float32)
    return lax.dot_general(
        flat_hot,
        flat_grad,
        (((0,), (0,)), ((), ())),
        precision=precise,
        preferred_element_type=jnp.float32,
    )


def shards(
    trunk_input,
    tokens,
    token_table,
    conv_weight,
    out_weight,
    norm_gain,
    mid_gain,
    strand_perm,
    dilation,
    out_cotangent,
):
    channels = trunk_input.shape[2]
    length = trunk_input.shape[1]
    inverse = (
        jnp.zeros((channels,), jnp.int32).at[strand_perm].set(jnp.arange(channels, dtype=jnp.int32))
    )
    one_hot = (tokens[..., None] == jnp.arange(4, dtype=jnp.int32)).astype(jnp.float32)
    hidden = (trunk_input.astype(jnp.float32) + embed(one_hot, token_table)).astype(jnp.bfloat16)
    saved = []
    for block_index in range(LAYERS):
        dilate = dilation[block_index]
        conv_main = conv_weight[block_index]
        out_main = out_weight[block_index]
        gain_main = norm_gain[block_index]
        mid_scale = mid_gain[block_index]
        other = reverse_strand(hidden, strand_perm)
        conv_other = conv_main
        out_other = out_main
        gain_other = gain_main
        padded_pair = halo_pair(jnp.stack([front(hidden, gain_main), front(other, gain_other)]))
        mid_a = middle(padded_pair[0], conv_main, dilate, length)
        mid_b = middle(padded_pair[1], conv_other, dilate, length)
        result_a = settle(finish(mid_a, out_main, mid_scale))
        rounded_b = lax.optimization_barrier(
            finish(mid_b, out_other, mid_scale).astype(jnp.bfloat16)
        )
        returned_b = restore_strand(rounded_b, inverse).astype(jnp.float32)
        saved.append((hidden, other, padded_pair, mid_a, mid_b, conv_other, out_other, gain_other))
        hidden = (hidden.astype(jnp.float32) + 0.5 * (result_a + returned_b)).astype(jnp.bfloat16)
    grad = out_cotangent
    conv_list = [None] * LAYERS
    out_list = [None] * LAYERS
    gain_list = [None] * LAYERS
    mid_list = [None] * LAYERS
    table_total = None
    for block_index in reversed(range(LAYERS)):
        dilate = dilation[block_index]
        conv_main = conv_weight[block_index]
        out_main = out_weight[block_index]
        gain_main = norm_gain[block_index]
        mid_scale = mid_gain[block_index]
        hidden_in, other, padded_pair, mid_a, mid_b, conv_other, out_other, gain_other = saved[
            block_index
        ]
        cotangent = (0.5 * grad.astype(jnp.float32)).astype(jnp.bfloat16)
        cotangent_b = reverse_strand(cotangent, strand_perm)
        dm_a, dwo_a, dmg_a = grad_back(mid_a, cotangent, out_main, mid_scale)
        dm_b, dwo_b, dmg_b = grad_back(mid_b, cotangent_b, out_other, mid_scale)
        dm_padded = with_halo(jnp.stack([dm_a, dm_b]), (("ctx", 2),), DMAX)
        dh_a, dconv_a, dgain_a = grad_front(
            padded_pair[0], dm_padded[0], conv_main, dilate, length, hidden_in, gain_main
        )
        dh_b, dconv_b, dgain_b = grad_front(
            padded_pair[1], dm_padded[1], conv_other, dilate, length, other, gain_other
        )
        back_b = restore_strand(
            lax.optimization_barrier(dh_b.astype(jnp.bfloat16)), inverse
        ).astype(jnp.float32)
        conv_local = dconv_a + dconv_b
        out_local = dwo_a + dwo_b
        gain_local = dgain_a + dgain_b
        mid_local = dmg_a + dmg_b
        grad = (grad.astype(jnp.float32) + settle(dh_a) + back_b).astype(jnp.bfloat16)
        conv_list[block_index] = conv_local
        out_list[block_index] = out_local
        gain_list[block_index] = gain_local
        mid_list[block_index] = mid_local
    table_local = table_term(one_hot, grad)
    conv_total, out_total, gain_total, mid_total, table_total = lax.psum(
        (
            jnp.stack(conv_list),
            jnp.stack(out_list),
            jnp.stack(gain_list),
            jnp.stack(mid_list),
            table_local,
        ),
        ("dp", "ctx"),
    )
    return (hidden, grad, table_total, conv_total, out_total, gain_total, mid_total)


def solution(mesh):
    placed = (
        P("dp", "ctx", None),
        P("dp", "ctx"),
        P(),
        P(),
        P(),
        P(),
        P(),
        P(),
        P(),
        P("dp", "ctx", None),
    )
    return jax.shard_map(
        shards,
        mesh=mesh,
        in_specs=placed,
        out_specs=(P("dp", "ctx", None), P("dp", "ctx", None), P(), P(), P(), P(), P()),
        check_vma=False,
    )
```

profile of v0, /device:TPU:1, one launch (start us, length us, event | category | flops | bytes accessed | tf_op | source)
XLA Modules:
  0.0 668.2 jit_solution(6969176788188938010)
XLA Ops:
  12.1 8.3 %collective-permute-done = bf16[1,256,768]{2,1,0:T(8,128)(2,1)S(1)} collective-permute-done((bf16[1,256,768]{2,1,0:T(8,128)(2,1)S(1)}, bf16[1,256,768]{2,1,0:T(8,128)(2,1)S(1)}, u32[]{:S(2)}, u32[]{:S(2)}) %collective-permute-start) | collective-permute-done | bytes 393248 | tf_op jit(solution)/shard_map/ppermute | solution.py:28
  23.6 7.6 %collective-permute-done.1 = bf16[1,256,768]{2,1,0:T(8,128)(2,1)S(1)} collective-permute-done((bf16[1,256,768]{2,1,0:T(8,128)(2,1)S(1)}, bf16[1,256,768]{2,1,0:T(8,128)(2,1)S(1)}, u32[]{:S(2)}, u32[]{:S(2)}) %collective-permute-start.1) | collective-permute-done | bytes 393248 | tf_op jit(solution)/shard_map/ppermute | solution.py:28
  88.1 6.3 rev.25
  104.2 8.9 %collective-permute-done.8 = bf16[1,256,768]{2,1,0:T(8,128)(2,1)S(1)} collective-permute-done((bf16[1,256,768]{2,1,0:T(8,128)(2,1)S(1)}, bf16[1,256,768]{2,1,0:T(8,128)(2,1)S(1)}, u32[]{:S(2)}, u32[]{:S(2)}) %collective-permute-start.8) | collective-permute-done | bytes 393248 | tf_op jit(solution)/shard_map/ppermute | solution.py:28
  126.8 6.3 rev.28
  151.6 6.3 rev.26
  170.4 5.5 collective-permute-done.13
  188.9 8.3 %collective-permute-done.15 = bf16[1,256,768]{2,1,0:T(8,128)(2,1)S(1)} collective-permute-done((bf16[1,256,768]{2,1,0:T(8,128)(2,1)S(1)}, bf16[1,256,768]{2,1,0:T(8,128)(2,1)S(1)}, u32[]{:S(2)}, u32[]{:S(2)}) %collective-permute-start.15) | collective-permute-done | bytes 393248 | tf_op jit(solution)/shard_map/ppermute | solution.py:28
  215.3 6.0 fusion.179
  252.1 6.4 rev.27
  295.5 9.8 %collective-permute-start.23 = (bf16[1,256,768]{2,1,0:T(8,128)(2,1)S(1)}, bf16[1,256,768]{2,1,0:T(8,128)(2,1)}, u32[]{:S(2)}, u32[]{:S(2)}) collective-permute-start(bf16[1,256,768]{2,1,0:T(8,128)(2,1)S(1)} %collective-permute-done.22), channel_id=1, source_target_pairs={{0,16},{1,17},{2,18},{3,19},{4,20},{5,21},{6,22},{7,23},{8,24},{9,... | collective-permute-start | bytes 1179656 | tf_op jit(solution)/shard_map/ppermute | solution.py:28
  323.6 6.4 rev.29
  330.8 6.0 collective-permute-done.31
  336.8 8.1 %collective-permute-done.32 = bf16[1,256,768]{2,1,0:T(8,128)(2,1)S(1)} collective-permute-done((bf16[1,256,768]{2,1,0:T(8,128)(2,1)S(1)}, bf16[1,256,768]{2,1,0:T(8,128)(2,1)S(1)}, u32[]{:S(2)}, u32[]{:S(2)}) %collective-permute-start.32) | collective-permute-done | bytes 393248 | tf_op jit(solution)/shard_map/ppermute | solution.py:28
  351.9 8.4 %collective-permute-done.34 = bf16[1,256,768]{2,1,0:T(8,128)(2,1)S(1)} collective-permute-done((bf16[1,256,768]{2,1,0:T(8,128)(2,1)S(1)}, bf16[1,256,768]{2,1,0:T(8,128)(2,1)S(1)}, u32[]{:S(2)}, u32[]{:S(2)}) %collective-permute-start.34) | collective-permute-done | bytes 393248 | tf_op jit(solution)/shard_map/ppermute | solution.py:28
  377.3 6.3 rev.30
  384.2 6.3 collective-permute-done.36
  407.2 6.3 collective-permute-done.39
  459.9 6.5 collective-permute-done.43
  477.4 5.5 collective-permute-done.45
  495.5 8.6 %collective-permute-done.47 = bf16[1,256,768]{2,1,0:T(8,128)(2,1)S(1)} collective-permute-done((bf16[1,256,768]{2,1,0:T(8,128)(2,1)S(1)}, bf16[1,256,768]{2,1,0:T(8,128)(2,1)S(1)}, u32[]{:S(2)}, u32[]{:S(2)}) %collective-permute-start.47) | collective-permute-done | bytes 393248 | tf_op jit(solution)/shard_map/ppermute | solution.py:28
  507.5 107.5 %all-reduce = (f32[4,768]{1,0:T(4,128)}, f32[2,768]{1,0:T(2,128)}, f32[2,384]{1,0:T(2,128)}) all-reduce(f32[4,768]{1,0:T(4,128)S(1)} %fusion.182, f32[2,768]{1,0:T(2,128)S(1)} %pad_maximum_fusion.14, f32[2,384]{1,0:T(2,128)S(1)} %pad_maximum_fusion.15), channel_id=1, replica_groups=mesh['dp'=4,'ctx'=32] {'dp','ctx'}, use_global_device_ids=true, to_apply=%region_33.35 | all-reduce | flops 5376 | bytes 43008 | tf_op jit(solution)/shard_map/psum | solution.py:233
  615.0 37.9 %all-reduce.4.cloned.1.call-done = (f32[2,3,768,384]{3,2,1,0:T(8,128)}, f32[2,384,768]{2,1,0:T(8,128)}) async-done(((f32[2,3,768,384]{3,2,1,0:T(8,128)}, f32[2,384,768]{2,1,0:T(8,128)}), (f32[2,3,768,384]{3,2,1,0:T(8,128)}, f32[2,384,768]{2,1,0:T(8,128)})) %all-reduce.4.cloned.1.call-update) | async-done | bytes 9437200 | tf_op jit(solution)/shard_map/psum | solution.py:233
  653.0 6.6 copy.47
  (486 shorter events, 346.2 us)
Async XLA Ops:
  7.2 645.8 %all-reduce.4.cloned.1.call-start = ((), (), s32[]{:S(2)}) async-start(), calls=%async_computation | async-start | bytes 18874368 | tf_op jit(solution)/shard_map/psum | solution.py:233
  10.0 10.5 %collective-permute-start = (bf16[1,256,768]{2,1,0:T(8,128)(2,1)S(1)}, bf16[1,256,768]{2,1,0:T(8,128)(2,1)S(1)}, u32[]{:S(2)}, u32[]{:S(2)}) collective-permute-start(bf16[1,256,768]{2,1,0:T(8,128)(2,1)S(1)} %rev.24), channel_id=1, source_target_pairs={{0,1},{1,0},{2,3},{3,2},{4,5},{5,4},{6,7},{7,6},{8,9},{9,8},{10,11... | collective-permute-start | bytes 1179656 | tf_op jit(solution)/shard_map/ppermute | solution.py:28
  20.4 10.8 %collective-permute-start.1 = (bf16[1,256,768]{2,1,0:T(8,128)(2,1)S(1)}, bf16[1,256,768]{2,1,0:T(8,128)(2,1)S(1)}, u32[]{:S(2)}, u32[]{:S(2)}) collective-permute-start(bf16[1,256,768]{2,1,0:T(8,128)(2,1)S(1)} %collective-permute-done), channel_id=1, source_target_pairs={{0,2},{1,3},{2,0},{3,1},{4,6},{5,7},{6,4},{7,5},{8,10},{9,11},{10,... | collective-permute-start | bytes 1179656 | tf_op jit(solution)/shard_map/ppermute | solution.py:28
  31.2 8.8 %collective-permute-start.2 = (bf16[1,256,768]{2,1,0:T(8,128)(2,1)S(1)}, bf16[1,256,768]{2,1,0:T(8,128)(2,1)S(1)}, u32[]{:S(2)}, u32[]{:S(2)}) collective-permute-start(bf16[1,256,768]{2,1,0:T(8,128)(2,1)S(1)} %collective-permute-done.1), channel_id=1, source_target_pairs={{0,4},{1,5},{2,6},{3,7},{4,0},{5,1},{6,2},{7,3},{8,12},{9,13},{10,... | collective-permute-start | bytes 1179656 | tf_op jit(solution)/shard_map/ppermute | solution.py:28
  40.1 11.7 %collective-permute-start.3 = (bf16[1,256,768]{2,1,0:T(8,128)(2,1)S(1)}, bf16[1,256,768]{2,1,0:T(8,128)(2,1)S(1)}, u32[]{:S(2)}, u32[]{:S(2)}) collective-permute-start(bf16[1,256,768]{2,1,0:T(8,128)(2,1)S(1)} %collective-permute-done.2), channel_id=1, source_target_pairs={{0,8},{1,9},{2,10},{3,11},{4,12},{5,13},{6,14},{7,15},{8,0},{9,1},... | collective-permute-start | bytes 1179656 | tf_op jit(solution)/shard_map/ppermute | solution.py:28
  68.2 8.5 %collective-permute-start.5 = (bf16[2,1,64,768]{3,2,1,0:T(8,128)(2,1)S(1)}, bf16[2,1,64,768]{3,2,1,0:T(8,128)(2,1)S(1)}, u32[]{:S(2)}, u32[]{:S(2)}) collective-permute-start(bf16[2,1,64,768]{3,2,1,0:T(8,128)(2,1)S(1)} %get-tuple-element.75), channel_id=1, source_target_pairs={{0,1},{1,2},{2,3},{3,4},{4,5},{5,6},{6,7},{7,8},{8,9},{9,10},{10,1... | collective-permute-start | bytes 589832 | tf_op jit(solution)/shard_map/ppermute | solution.py:19
  101.3 11.9 %collective-permute-start.8 = (bf16[1,256,768]{2,1,0:T(8,128)(2,1)S(1)}, bf16[1,256,768]{2,1,0:T(8,128)(2,1)S(1)}, u32[]{:S(2)}, u32[]{:S(2)}) collective-permute-start(bf16[1,256,768]{2,1,0:T(8,128)(2,1)S(1)} %collective-permute-done.7), channel_id=1, source_target_pairs={{0,2},{1,3},{2,0},{3,1},{4,6},{5,7},{6,4},{7,5},{8,10},{9,11},{10,... | collective-permute-start | bytes 1179656 | tf_op jit(solution)/shard_map/ppermute | solution.py:28
  120.3 13.5 %collective-permute-start.10 = (bf16[1,256,768]{2,1,0:T(8,128)(2,1)}, bf16[1,256,768]{2,1,0:T(8,128)(2,1)}, u32[]{:S(2)}, u32[]{:S(2)}) collective-permute-start(bf16[1,256,768]{2,1,0:T(8,128)(2,1)} %collective-permute-done.9), channel_id=1, source_target_pairs={{0,8},{1,9},{2,10},{3,11},{4,12},{5,13},{6,14},{7,15},{8,0},{9,1},... | collective-permute-start | bytes 1179656 | tf_op jit(solution)/shard_map/ppermute | solution.py:28
  133.2 25.5 %collective-permute-start.24 = (bf16[1,256,768]{2,1,0:T(8,128)(2,1)}, bf16[1,256,768]{2,1,0:T(8,128)(2,1)}, u32[]{:S(2)}, u32[]{:S(2)}) collective-permute-start(bf16[1,256,768]{2,1,0:T(8,128)(2,1)} %rev.28), channel_id=1, source_target_pairs={{0,1},{1,0},{2,3},{3,2},{4,5},{5,4},{6,7},{7,6},{8,9},{9,8},{10,11... | collective-permute-start | bytes 1179656 | tf_op jit(solution)/shard_map/ppermute | solution.py:28
  158.7 11.7 %collective-permute-start.25 = (bf16[1,256,768]{2,1,0:T(8,128)(2,1)}, bf16[1,256,768]{2,1,0:T(8,128)(2,1)S(1)}, u32[]{:S(2)}, u32[]{:S(2)}) collective-permute-start(bf16[1,256,768]{2,1,0:T(8,128)(2,1)} %collective-permute-done.24), channel_id=1, source_target_pairs={{0,2},{1,3},{2,0},{3,1},{4,6},{5,7},{6,4},{7,5},{8,10},{9,11},{10,... | collective-permute-start | bytes 1179656 | tf_op jit(solution)/shard_map/ppermute | solution.py:28
  164.8 11.1 %collective-permute-start.13 = (bf16[1,256,768]{2,1,0:T(8,128)(2,1)S(1)}, bf16[1,256,768]{2,1,0:T(8,128)(2,1)S(1)}, u32[]{:S(2)}, u32[]{:S(2)}) collective-permute-start(bf16[1,256,768]{2,1,0:T(8,128)(2,1)S(1)} %collective-permute-done.12), channel_id=1, source_target_pairs={{0,2},{1,3},{2,0},{3,1},{4,6},{5,7},{6,4},{7,5},{8,10},{9,11},{10,... | collective-permute-start | bytes 1179656 | tf_op jit(solution)/shard_map/ppermute | solution.py:28
  177.3 11.6 %collective-permute-start.27 = (bf16[1,256,768]{2,1,0:T(8,128)(2,1)S(1)}, bf16[1,256,768]{2,1,0:T(8,128)(2,1)}, u32[]{:S(2)}, u32[]{:S(2)}) collective-permute-start(bf16[1,256,768]{2,1,0:T(8,128)(2,1)S(1)} %collective-permute-done.26), channel_id=1, source_target_pairs={{0,8},{1,9},{2,10},{3,11},{4,12},{5,13},{6,14},{7,15},{8,0},{9,1},... | collective-permute-start | bytes 1179656 | tf_op jit(solution)/shard_map/ppermute | solution.py:28
  182.8 14.4 %collective-permute-start.15 = (bf16[1,256,768]{2,1,0:T(8,128)(2,1)S(1)}, bf16[1,256,768]{2,1,0:T(8,128)(2,1)S(1)}, u32[]{:S(2)}, u32[]{:S(2)}) collective-permute-start(bf16[1,256,768]{2,1,0:T(8,128)(2,1)S(1)} %collective-permute-done.14), channel_id=1, source_target_pairs={{0,8},{1,9},{2,10},{3,11},{4,12},{5,13},{6,14},{7,15},{8,0},{9,1},... | collective-permute-start | bytes 1179656 | tf_op jit(solution)/shard_map/ppermute | solution.py:28
  188.9 39.9 %collective-permute-start.28 = (bf16[1,256,768]{2,1,0:T(8,128)(2,1)}, bf16[1,256,768]{2,1,0:T(8,128)(2,1)}, u32[]{:S(2)}, u32[]{:S(2)}) collective-permute-start(bf16[1,256,768]{2,1,0:T(8,128)(2,1)} %collective-permute-done.27), channel_id=1, source_target_pairs={{0,16},{1,17},{2,18},{3,19},{4,20},{5,21},{6,22},{7,23},{8,24},{9,... | collective-permute-start | bytes 1179656 | tf_op jit(solution)/shard_map/ppermute | solution.py:28
  222.8 11.8 %collective-permute-start.17 = (bf16[2,1,64,768]{3,2,1,0:T(8,128)(2,1)}, bf16[2,1,64,768]{3,2,1,0:T(8,128)(2,1)}, u32[]{:S(2)}, u32[]{:S(2)}) collective-permute-start(bf16[2,1,64,768]{3,2,1,0:T(8,128)(2,1)} %get-tuple-element.73), channel_id=1, source_target_pairs={{0,1},{1,2},{2,3},{3,4},{4,5},{5,6},{6,7},{7,8},{8,9},{9,10},{10,1... | collective-permute-start | bytes 589832 | tf_op jit(solution)/shard_map/ppermute | solution.py:19
  224.8 9.8 %collective-permute-start.18 = (bf16[2,1,64,768]{3,2,1,0:T(8,128)(2,1)}, bf16[2,1,64,768]{3,2,1,0:T(8,128)(2,1)}, u32[]{:S(2)}, u32[]{:S(2)}) collective-permute-start(bf16[2,1,64,768]{3,2,1,0:T(8,128)(2,1)} %get-tuple-element.74), channel_id=1, source_target_pairs={{1,0},{2,1},{3,2},{4,3},{5,4},{6,5},{7,6},{8,7},{9,8},{10,9},{11,1... | collective-permute-start | bytes 589832 | tf_op jit(solution)/shard_map/ppermute | solution.py:22
  245.0 18.0 %collective-permute-start.29 = (bf16[2,1,64,384]{3,2,1,0:T(8,128)(2,1)}, bf16[2,1,64,384]{3,2,1,0:T(8,128)(2,1)}, u32[]{:S(2)}, u32[]{:S(2)}) collective-permute-start(bf16[2,1,64,384]{3,2,1,0:T(8,128)(2,1)} %get-tuple-element.88), channel_id=1, source_target_pairs={{0,1},{1,2},{2,3},{3,4},{4,5},{5,6},{6,7},{7,8},{8,9},{9,10},{10,1... | collective-permute-start | bytes 294920 | tf_op jit(solution)/shard_map/ppermute | solution.py:19
  249.6 13.4 %collective-permute-start.30 = (bf16[2,1,64,384]{3,2,1,0:T(8,128)(2,1)}, bf16[2,1,64,384]{3,2,1,0:T(8,128)(2,1)}, u32[]{:S(2)}, u32[]{:S(2)}) collective-permute-start(bf16[2,1,64,384]{3,2,1,0:T(8,128)(2,1)} %get-tuple-element.89), channel_id=1, source_target_pairs={{1,0},{2,1},{3,2},{4,3},{5,4},{6,5},{7,6},{8,7},{9,8},{10,9},{11,1... | collective-permute-start | bytes 294920 | tf_op jit(solution)/shard_map/ppermute | solution.py:22
  277.3 10.1 %collective-permute-start.21 = (bf16[1,256,768]{2,1,0:T(8,128)(2,1)S(1)}, bf16[1,256,768]{2,1,0:T(8,128)(2,1)S(1)}, u32[]{:S(2)}, u32[]{:S(2)}) collective-permute-start(bf16[1,256,768]{2,1,0:T(8,128)(2,1)S(1)} %collective-permute-done.20), channel_id=1, source_target_pairs={{0,4},{1,5},{2,6},{3,7},{4,0},{5,1},{6,2},{7,3},{8,12},{9,13},{10,... | collective-permute-start | bytes 1179656 | tf_op jit(solution)/shard_map/ppermute | solution.py:28
  295.5 15.3 %collective-permute-start.23 = (bf16[1,256,768]{2,1,0:T(8,128)(2,1)S(1)}, bf16[1,256,768]{2,1,0:T(8,128)(2,1)}, u32[]{:S(2)}, u32[]{:S(2)}) collective-permute-start(bf16[1,256,768]{2,1,0:T(8,128)(2,1)S(1)} %collective-permute-done.22), channel_id=1, source_target_pairs={{0,16},{1,17},{2,18},{3,19},{4,20},{5,21},{6,22},{7,23},{8,24},{9,... | collective-permute-start | bytes 1179656 | tf_op jit(solution)/shard_map/ppermute | solution.py:28
  351.9 8.4 %collective-permute-start.34 = (bf16[1,256,768]{2,1,0:T(8,128)(2,1)S(1)}, bf16[1,256,768]{2,1,0:T(8,128)(2,1)S(1)}, u32[]{:S(2)}, u32[]{:S(2)}) collective-permute-start(bf16[1,256,768]{2,1,0:T(8,128)(2,1)S(1)} %collective-permute-done.33), channel_id=1, source_target_pairs={{0,8},{1,9},{2,10},{3,11},{4,12},{5,13},{6,14},{7,15},{8,0},{9,1},... | collective-permute-start | bytes 1179656 | tf_op jit(solution)/shard_map/ppermute | solution.py:28
  466.4 10.0 %collective-permute-start.44 = (bf16[1,256,768]{2,1,0:T(8,128)(2,1)S(1)}, bf16[1,256,768]{2,1,0:T(8,128)(2,1)S(1)}, u32[]{:S(2)}, u32[]{:S(2)}) collective-permute-start(bf16[1,256,768]{2,1,0:T(8,128)(2,1)S(1)} %collective-permute-done.43), channel_id=1, source_target_pairs={{0,2},{1,3},{2,0},{3,1},{4,6},{5,7},{6,4},{7,5},{8,10},{9,11},{10,... | collective-permute-start | bytes 1179656 | tf_op jit(solution)/shard_map/ppermute | solution.py:28
  483.0 9.8 %collective-permute-start.46 = (bf16[1,256,768]{2,1,0:T(8,128)(2,1)S(1)}, bf16[1,256,768]{2,1,0:T(8,128)(2,1)S(1)}, u32[]{:S(2)}, u32[]{:S(2)}) collective-permute-start(bf16[1,256,768]{2,1,0:T(8,128)(2,1)S(1)} %collective-permute-done.45), channel_id=1, source_target_pairs={{0,8},{1,9},{2,10},{3,11},{4,12},{5,13},{6,14},{7,15},{8,0},{9,1},... | collective-permute-start | bytes 1179656 | tf_op jit(solution)/shard_map/ppermute | solution.py:28
  492.8 11.3 %collective-permute-start.47 = (bf16[1,256,768]{2,1,0:T(8,128)(2,1)S(1)}, bf16[1,256,768]{2,1,0:T(8,128)(2,1)S(1)}, u32[]{:S(2)}, u32[]{:S(2)}) collective-permute-start(bf16[1,256,768]{2,1,0:T(8,128)(2,1)S(1)} %collective-permute-done.46), channel_id=1, source_target_pairs={{0,16},{1,17},{2,18},{3,19},{4,20},{5,21},{6,22},{7,23},{8,24},{9,... | collective-permute-start | bytes 1179656 | tf_op jit(solution)/shard_map/ppermute | solution.py:28
  (140 other events, 1213.5 us)
Sparse Core Ops, SparseCore 0:
  451.2 201.7 all-reduce.3
where the time goes:
time: 679 us; the launch traced here: 668 us
  waiting for transfers between devices  233 us (34%)
  local copies, waits for them, and re-layouts  112 us (16%)
  blocking collectives  108 us (16%)
  starting transfers between devices  94 us (14%)
  other arithmetic  53.8 us (8%)
  matrix products  45.7 us (7%)
  between operations  21.6 us (3%)
    ppermute x40, waiting for transfers between devices, swapped(): lax.ppermute(value, axis, [(i, i ^ 1 << apart) for i in range(lax.axis_si...  192 us
    psum x1, blocking collectives, shards(): lax.psum((jnp.stack(conv_list), jnp.stack(out_list), jnp.stack(gain_list)...  108 us
    ppermute x40, starting transfers between devices, swapped(): lax.ppermute(value, axis, [(i, i ^ 1 << apart) for i in range(lax.axis_si...  76.3 us
    rev x8, local copies, waits for them, and re-layouts, mirror_bins(): flipped = values[:, ::-1]  39.1 us
    psum x1, waiting for transfers between devices, shards(): lax.psum((jnp.stack(conv_list), jnp.stack(out_list), jnp.stack(gain_list)...  37.9 us
    dot_general x16, matrix products, matmul_t(): lax.dot_general(flat, right, (((1,), (1,)), ((), ())), preferred_element_...  21.5 us
    gather x8, local copies, waits for them, and re-layouts, restore_strand(): return jnp.take(mirror_bins(values), inverse, axis=2)  20.3 us
    unnamed x232, local copies, waits for them, and re-layouts  17.9 us
  transfers between devices with their start and end apart: 49, of which 40 were waited for; matrix products, arithmetic and copies ran while one was open for 16% of the time, Pallas kernels for 0%

commit v1 on v0

--- a/solution.py
+++ b/solution.py
@@ -22,10 +22,6 @@
         high = lax.ppermute(lax.slice_in_dim(block, 0, width, axis=dim), axis, backward)
         block = jnp.concatenate([low, block, high], axis=dim)
     return block
-
-
-def swapped(value, axis, apart):
-    return lax.ppermute(value, axis, [(i, i ^ 1 << apart) for i in range(lax.axis_size(axis))])
 
 
 def normed_act(values, scaling):
@@ -117,20 +113,17 @@
     return (d_hidden, d_conv, d_scaling)
 
 
-def mirror_bins(values):
-    flipped = values[:, ::-1]
-    bit_count = lax.axis_size("ctx").bit_length() - 1
-    for bit_index in range(bit_count):
-        flipped = swapped(flipped, "ctx", bit_index)
-    return flipped
-
-
-def reverse_strand(values, strand_perm):
-    return jnp.take(mirror_bins(values), strand_perm, axis=2)
-
-
-def restore_strand(values, inverse):
-    return jnp.take(mirror_bins(values), inverse, axis=2)
+def channel_matrix(strand_perm):
+    rows = jnp.arange(strand_perm.shape[0], dtype=jnp.int32)[:, None]
+    return (rows == strand_perm[None, :]).astype(jnp.bfloat16)
+
+
+def relabel(values, matrix):
+    return matmul(values, matrix).astype(jnp.bfloat16)
+
+
+def relabel_back(values, matrix):
+    return matmul_t(values, matrix).astype(jnp.bfloat16)
 
 
 def embed(one_hot, token_table):
@@ -163,11 +156,8 @@
     dilation,
     out_cotangent,
 ):
-    channels = trunk_input.shape[2]
     length = trunk_input.shape[1]
-    inverse = (
-        jnp.zeros((channels,), jnp.int32).at[strand_perm].set(jnp.arange(channels, dtype=jnp.int32))
-    )
+    matrix = channel_matrix(strand_perm)
     one_hot = (tokens[..., None] == jnp.arange(4, dtype=jnp.int32)).astype(jnp.float32)
     hidden = (trunk_input.astype(jnp.float32) + embed(one_hot, token_table)).astype(jnp.bfloat16)
     saved = []
@@ -177,8 +167,8 @@
         out_main = out_weight[block_index]
         gain_main = norm_gain[block_index]
         mid_scale = mid_gain[block_index]
-        other = reverse_strand(hidden, strand_perm)
-        conv_other = conv_main
+        other = relabel(hidden, matrix)
+        conv_other = conv_main[::-1]
         out_other = out_main
         gain_other = gain_main
         padded_pair = halo_pair(jnp.stack([front(hidden, gain_main), front(other, gain_other)]))
@@ -188,7 +178,7 @@
         rounded_b = lax.optimization_barrier(
             finish(mid_b, out_other, mid_scale).astype(jnp.bfloat16)
         )
-        returned_b = restore_strand(rounded_b, inverse).astype(jnp.float32)
+        returned_b = relabel_back(rounded_b, matrix).astype(jnp.float32)
         saved.append((hidden, other, padded_pair, mid_a, mid_b, conv_other, out_other, gain_other))
         hidden = (hidden.astype(jnp.float32) + 0.5 * (result_a + returned_b)).astype(jnp.bfloat16)
     grad = out_cotangent
@@ -207,7 +197,7 @@
             block_index
         ]
         cotangent = (0.5 * grad.astype(jnp.float32)).astype(jnp.bfloat16)
-        cotangent_b = reverse_strand(cotangent, strand_perm)
+        cotangent_b = relabel(cotangent, matrix)
         dm_a, dwo_a, dmg_a = grad_back(mid_a, cotangent, out_main, mid_scale)
         dm_b, dwo_b, dmg_b = grad_back(mid_b, cotangent_b, out_other, mid_scale)
         dm_padded = with_halo(jnp.stack([dm_a, dm_b]), (("ctx", 2),), DMAX)
@@ -217,10 +207,10 @@
         dh_b, dconv_b, dgain_b = grad_front(
             padded_pair[1], dm_padded[1], conv_other, dilate, length, other, gain_other
         )
-        back_b = restore_strand(
-            lax.optimization_barrier(dh_b.astype(jnp.bfloat16)), inverse
+        back_b = relabel_back(
+            lax.optimization_barrier(dh_b.astype(jnp.bfloat16)), matrix
         ).astype(jnp.float32)
-        conv_local = dconv_a + dconv_b
+        conv_local = dconv_a + dconv_b[::-1]
         out_local = dwo_a + dwo_b
         gain_local = dgain_a + dgain_b
         mid_local = dmg_a + dmg_b

time: 679 us -> 302 us (0.44)
  waiting for transfers between devices: 233 us -> 95.3 us
  local copies, waits for them, and re-layouts: 112 us -> 14.9 us
  starting transfers between devices: 94 us -> 23.5 us
  other arithmetic: 53.8 us -> 26.5 us
  blocking collectives: 108 us -> 81 us
  matrix products: 45.7 us -> 35.3 us
    ppermute x40 -> x0, waiting for transfers between devices: 192 us -> none  [swapped(): lax.ppermute(value, axis, [(i, i ^ 1 << apart) for i in range(lax.axis_si...]
    ppermute x40 -> x0, starting transfers between devices: 76.3 us -> none  [swapped(): lax.ppermute(value, axis, [(i, i ^ 1 << apart) for i in range(lax.axis_si...]
    psum x1, waiting for transfers between devices: 37.9 us -> 86.7 us  [shards(): lax.psum((jnp.stack(conv_list), jnp.stack(out_list), jnp.stack(gain_list)...]
    rev x8 -> x0, local copies, waits for them, and re-layouts: 39.1 us -> none  [mirror_bins(): flipped = values[:, ::-1]]
    gather x14 -> x0, local copies, waits for them, and re-layouts: 36.7 us -> none  [the longest x8 20.3 us: restore_strand(): return jnp.take(mirror_bins(values), inverse, axis=2)]
    psum x1, blocking collectives: 108 us -> 81 us  [shards(): lax.psum((jnp.stack(conv_list), jnp.stack(out_list), jnp.stack(gain_list)...]
    another operation x8 -> x0, local copies, waits for them, and re-layouts: 11.9 us -> none  [the longest x4 5.95 us: restore_strand(): return jnp.take(mirror_bins(values), inverse, axis=2)]
    dot_general x16 -> x20, matrix products: 21.5 us -> 15.4 us  [matmul_t(): lax.dot_general(flat, right, (((1,), (1,)), ((), ())), preferred_element_...]
  transfers between devices with their start and end apart: 49 -> 9, of which waited for: 40 -> 5; matrix products, arithmetic and copies ran while one was open for 16% -> 5% of each run, Pallas kernels for 0% -> 0%
where the time goes in v1:
time: 302 us; the launch traced here: 297 us
  waiting for transfers between devices  95.3 us (32%)
  blocking collectives  81 us (27%)
  matrix products  35.3 us (12%)
  other arithmetic  26.5 us (9%)
  starting transfers between devices  23.5 us (8%)
  between operations  20.6 us (7%)
  local copies, waits for them, and re-layouts  14.9 us (5%)
    psum x1, waiting for transfers between devices, shards(): lax.psum((jnp.stack(conv_list), jnp.stack(out_list), jnp.stack(gain_list)...  86.7 us
    psum x1, blocking collectives, shards(): lax.psum((jnp.stack(conv_list), jnp.stack(out_list), jnp.stack(gain_list)...  81 us
    ppermute x4, starting transfers between devices, with_halo(): lax.ppermute(lax.slice_in_dim(block, block.shape[dim] - width, None, axis...  17.1 us
    dot_general x20, matrix products, matmul_t(): lax.dot_general(flat, right, (((1,), (1,)), ((), ())), preferred_element_...  15.4 us
    unnamed x86, local copies, waits for them, and re-layouts  12.1 us
    dot_general x20, matrix products, matmul(): product = jnp.dot(flat, right, preferred_element_type=jnp.float32)  11.7 us
    another operation x4, other arithmetic, shards(): jnp.stack([front(hidden, gain_main), front(other, gain_other)])  9.54 us
    ppermute x4, waiting for transfers between devices, with_halo(): lax.ppermute(lax.slice_in_dim(block, 0, width, axis=dim), axis, backward)  8.19 us
  transfers between devices with their start and end apart: 9, of which 5 were waited for; matrix products, arithmetic and copies ran while one was open for 5% of the time, Pallas kernels for 0%

profile of v1, /device:TPU:1, one launch (start us, length us, event | category | flops | bytes accessed | tf_op | source)
XLA Modules:
  0.0 296.9 jit_solution(1994809795893420637)
XLA Ops:
  8.0 1.6 convert_reduce_fusion.1
  12.8 2.8 fusion.174
  15.6 2.8 fusion.180
  18.5 4.0 %collective-permute-start = (bf16[2,1,64,768]{3,2,1,0:T(8,128)(2,1)S(1)}, bf16[2,1,64,768]{3,2,1,0:T(8,128)(2,1)S(1)}, u32[]{:S(2)}, u32[]{:S(2)}) collective-permute-start(bf16[2,1,64,768]{3,2,1,0:T(8,128)(2,1)S(1)} %get-tuple-element.74), channel_id=1, source_target_pairs={{0,1},{1,2},{2,3},{3,4},{4,5},{5,6},{6,7},{7,8},{8,9},{9,10},{10,1... | collective-permute-start | bytes 589832 | tf_op jit(solution)/shard_map/ppermute | solution.py:19
  22.5 1.6 collective-permute-start.1
  30.1 1.8 copy-done.2
  34.8 1.9 multiply_convert_fusion.5
  39.5 1.9 fusion.175
  41.5 1.9 fusion.181
  43.4 4.0 %collective-permute-start.2 = (bf16[2,1,64,768]{3,2,1,0:T(8,128)(2,1)S(1)}, bf16[2,1,64,768]{3,2,1,0:T(8,128)(2,1)S(1)}, u32[]{:S(2)}, u32[]{:S(2)}) collective-permute-start(bf16[2,1,64,768]{3,2,1,0:T(8,128)(2,1)S(1)} %get-tuple-element.72), channel_id=1, source_target_pairs={{0,1},{1,2},{2,3},{3,4},{4,5},{5,6},{6,7},{7,8},{8,9},{9,10},{10,1... | collective-permute-start | bytes 589832 | tf_op jit(solution)/shard_map/ppermute | solution.py:19
  47.4 1.8 collective-permute-start.3
  50.4 3.8 %collective-permute-done.3 = bf16[2,1,64,768]{3,2,1,0:T(8,128)(2,1)S(1)} collective-permute-done((bf16[2,1,64,768]{3,2,1,0:T(8,128)(2,1)S(1)}, bf16[2,1,64,768]{3,2,1,0:T(8,128)(2,1)S(1)}, u32[]{:S(2)}, u32[]{:S(2)}) %collective-permute-start.3) | collective-permute-done | bytes 196640 | tf_op jit(solution)/shard_map/ppermute | solution.py:22
  57.2 1.9 multiply_convert_fusion.3
  61.4 3.7 %collective-permute-start.4 = (bf16[2,1,64,384]{3,2,1,0:T(8,128)(2,1)S(1)}, bf16[2,1,64,384]{3,2,1,0:T(8,128)(2,1)S(1)}, u32[]{:S(2)}, u32[]{:S(2)}) collective-permute-start(bf16[2,1,64,384]{3,2,1,0:T(8,128)(2,1)S(1)} %get-tuple-element.86), channel_id=1, source_target_pairs={{0,1},{1,2},{2,3},{3,4},{4,5},{5,6},{6,7},{7,8},{8,9},{9,10},{10,1... | collective-permute-start | bytes 294920 | tf_op jit(solution)/shard_map/ppermute | solution.py:19
  68.5 3.2 %collective-permute-done.5 = bf16[2,1,64,384]{3,2,1,0:T(8,128)(2,1)S(1)} collective-permute-done((bf16[2,1,64,384]{3,2,1,0:T(8,128)(2,1)S(1)}, bf16[2,1,64,384]{3,2,1,0:T(8,128)(2,1)S(1)}, u32[]{:S(2)}, u32[]{:S(2)}) %collective-permute-start.5) | collective-permute-done | bytes 98336 | tf_op jit(solution)/shard_map/ppermute | solution.py:22
  83.8 5.4 %collective-permute-start.6 = (bf16[2,1,64,384]{3,2,1,0:T(8,128)(2,1)S(1)}, bf16[2,1,64,384]{3,2,1,0:T(8,128)(2,1)S(1)}, u32[]{:S(2)}, u32[]{:S(2)}) collective-permute-start(bf16[2,1,64,384]{3,2,1,0:T(8,128)(2,1)S(1)} %get-tuple-element.84), channel_id=1, source_target_pairs={{0,1},{1,2},{2,3},{3,4},{4,5},{5,6},{6,7},{7,8},{8,9},{9,10},{10,1... | collective-permute-start | bytes 294920 | tf_op jit(solution)/shard_map/ppermute | solution.py:19
  89.2 1.5 collective-permute-start.7
  91.8 1.6 pad_maximum_fusion.3
  98.8 3.4 %pad_maximum_fusion = f32[2,3,768,384]{3,2,1,0:T(8,128)} fusion(f32[1,3,768,384]{3,2,1,0:T(8,128)S(1)} %fusion.1, f32[1,3,768,384]{3,2,1,0:T(8,128)S(1)} %fusion), kind=kLoop, calls=%fused_computation | loop fusion | flops 1769472 | bytes 14155776 | tf_op jit(solution)/shard_map/stack | solution.py:225
  102.3 1.6 fusion.28
  104.6 2.6 fusion.44
  114.2 81.0 %all-reduce = (f32[4,768]{1,0:T(4,128)}, f32[2,768]{1,0:T(2,128)}, f32[2,384]{1,0:T(2,128)}) all-reduce(f32[4,768]{1,0:T(4,128)S(1)} %fusion.182, f32[2,768]{1,0:T(2,128)S(1)} %pad_maximum_fusion.16, f32[2,384]{1,0:T(2,128)S(1)} %copy-done.24), channel_id=1, replica_groups=mesh['dp'=4,'ctx'=32] {'dp','ctx'}, use_global_device_ids=true, to_apply=%region_32.0 | all-reduce | flops 5376 | bytes 43008 | tf_op jit(solution)/shard_map/psum | solution.py:223
  195.2 86.7 %all-reduce.4.cloned.1.call-done = (f32[2,3,768,384]{3,2,1,0:T(8,128)}, f32[2,384,768]{2,1,0:T(8,128)}) async-done(((f32[2,3,768,384]{3,2,1,0:T(8,128)}, f32[2,384,768]{2,1,0:T(8,128)}), (f32[2,3,768,384]{3,2,1,0:T(8,128)}, f32[2,384,768]{2,1,0:T(8,128)})) %all-reduce.4.cloned.1.call-update) | async-done | bytes 9437200 | tf_op jit(solution)/shard_map/psum | solution.py:223
  281.9 6.6 %copy.19 = f32[2,3,768,384]{3,2,1,0:T(8,128)} copy(f32[2,3,768,384]{3,2,1,0:T(8,128)} %get-tuple-element.129) | data formatting | bytes 14155776
  (230 shorter events, 47.2 us)
Async XLA Ops:
  7.2 274.7 %all-reduce.4.cloned.1.call-start = ((), (), s32[]{:S(2)}) async-start(), calls=%async_computation | async-start | bytes 18874368 | tf_op jit(solution)/shard_map/psum | solution.py:223
  9.7 5.9 %copy-start.5 = (bf16[1,256,768]{2,1,0:T(8,128)(2,1)}, bf16[1,256,768]{2,1,0:T(8,128)(2,1)S(1)}, u32[]{:S(2)}) copy-start(bf16[1,256,768]{2,1,0:T(8,128)(2,1)S(1)} %get-tuple-element.105) | copy-start | bytes 1179652
  10.5 5.2 %copy-start.25 = (f32[256]{0:T(256)}, f32[256]{0:T(256)S(1)}, u32[]{:S(2)}) copy-start(f32[256]{0:T(256)S(1)} %fusion.334) | copy-start | bytes 3076
  11.9 6.6 %copy-start.3 = (f32[256,768]{1,0:T(8,128)}, f32[256,768]{1,0:T(8,128)S(1)}, u32[]{:S(2)}) copy-start(f32[256,768]{1,0:T(8,128)S(1)} %get-tuple-element.103) | copy-start | bytes 2359300
  12.8 11.3 %copy-start.39 = (s32[2]{0:T(128)S(1)}, s32[2]{0:T(128)}, u32[]{:S(2)}) copy-start(s32[2]{0:T(128)} %param.18) | copy-start | bytes 28
  12.8 17.1 %copy-start.36 = (f32[2,384]{1,0:T(2,128)S(1)}, f32[2,384]{1,0:T(2,128)}, u32[]{:S(2)}) copy-start(f32[2,384]{1,0:T(2,128)} %param.16) | copy-start | bytes 9220
  18.5 11.4 %collective-permute-start = (bf16[2,1,64,768]{3,2,1,0:T(8,128)(2,1)S(1)}, bf16[2,1,64,768]{3,2,1,0:T(8,128)(2,1)S(1)}, u32[]{:S(2)}, u32[]{:S(2)}) collective-permute-start(bf16[2,1,64,768]{3,2,1,0:T(8,128)(2,1)S(1)} %get-tuple-element.74), channel_id=1, source_target_pairs={{0,1},{1,2},{2,3},{3,4},{4,5},{5,6},{6,7},{7,8},{8,9},{9,10},{10,1... | collective-permute-start | bytes 589832 | tf_op jit(solution)/shard_map/ppermute | solution.py:19
  22.5 7.4 %collective-permute-start.1 = (bf16[2,1,64,768]{3,2,1,0:T(8,128)(2,1)S(1)}, bf16[2,1,64,768]{3,2,1,0:T(8,128)(2,1)S(1)}, u32[]{:S(2)}, u32[]{:S(2)}) collective-permute-start(bf16[2,1,64,768]{3,2,1,0:T(8,128)(2,1)S(1)} %get-tuple-element.75), channel_id=1, source_target_pairs={{1,0},{2,1},{3,2},{4,3},{5,4},{6,5},{7,6},{8,7},{9,8},{10,9},{11,1... | collective-permute-start | bytes 589832 | tf_op jit(solution)/shard_map/ppermute | solution.py:22
  38.2 39.3 %copy-start.13 = (bf16[1,256,768]{2,1,0:T(8,128)(2,1)}, bf16[1,256,768]{2,1,0:T(8,128)(2,1)S(1)}, u32[]{:S(2)}) copy-start(bf16[1,256,768]{2,1,0:T(8,128)(2,1)S(1)} %get-tuple-element.113) | copy-start | bytes 1179652
  39.5 9.8 %copy-start.22 = (bf16[1,256,768]{2,1,0:T(8,128)(2,1)S(1)}, bf16[1,256,768]{2,1,0:T(8,128)(2,1)}, u32[]{:S(2)}) copy-start(bf16[1,256,768]{2,1,0:T(8,128)(2,1)} %param.19) | copy-start | bytes 1179652
  43.4 6.9 %collective-permute-start.2 = (bf16[2,1,64,768]{3,2,1,0:T(8,128)(2,1)S(1)}, bf16[2,1,64,768]{3,2,1,0:T(8,128)(2,1)S(1)}, u32[]{:S(2)}, u32[]{:S(2)}) collective-permute-start(bf16[2,1,64,768]{3,2,1,0:T(8,128)(2,1)S(1)} %get-tuple-element.72), channel_id=1, source_target_pairs={{0,1},{1,2},{2,3},{3,4},{4,5},{5,6},{6,7},{7,8},{8,9},{9,10},{10,1... | collective-permute-start | bytes 589832 | tf_op jit(solution)/shard_map/ppermute | solution.py:19
  47.4 6.8 %collective-permute-start.3 = (bf16[2,1,64,768]{3,2,1,0:T(8,128)(2,1)S(1)}, bf16[2,1,64,768]{3,2,1,0:T(8,128)(2,1)S(1)}, u32[]{:S(2)}, u32[]{:S(2)}) collective-permute-start(bf16[2,1,64,768]{3,2,1,0:T(8,128)(2,1)S(1)} %get-tuple-element.73), channel_id=1, source_target_pairs={{1,0},{2,1},{3,2},{4,3},{5,4},{6,5},{7,6},{8,7},{9,8},{10,9},{11,1... | collective-permute-start | bytes 589832 | tf_op jit(solution)/shard_map/ppermute | solution.py:22
  59.1 8.2 %copy-start.15 = (bf16[256,384]{1,0:T(8,128)(2,1)}, bf16[256,384]{1,0:T(8,128)(2,1)S(1)}, u32[]{:S(2)}) copy-start(bf16[256,384]{1,0:T(8,128)(2,1)S(1)} %get-tuple-element.96) | copy-start | bytes 589828
  61.4 7.1 %collective-permute-start.4 = (bf16[2,1,64,384]{3,2,1,0:T(8,128)(2,1)S(1)}, bf16[2,1,64,384]{3,2,1,0:T(8,128)(2,1)S(1)}, u32[]{:S(2)}, u32[]{:S(2)}) collective-permute-start(bf16[2,1,64,384]{3,2,1,0:T(8,128)(2,1)S(1)} %get-tuple-element.86), channel_id=1, source_target_pairs={{0,1},{1,2},{2,3},{3,4},{4,5},{5,6},{6,7},{7,8},{8,9},{9,10},{10,1... | collective-permute-start | bytes 294920 | tf_op jit(solution)/shard_map/ppermute | solution.py:19
  65.1 6.5 %collective-permute-start.5 = (bf16[2,1,64,384]{3,2,1,0:T(8,128)(2,1)S(1)}, bf16[2,1,64,384]{3,2,1,0:T(8,128)(2,1)S(1)}, u32[]{:S(2)}, u32[]{:S(2)}) collective-permute-start(bf16[2,1,64,384]{3,2,1,0:T(8,128)(2,1)S(1)} %get-tuple-element.87), channel_id=1, source_target_pairs={{1,0},{2,1},{3,2},{4,3},{5,4},{6,5},{7,6},{8,7},{9,8},{10,9},{11,1... | collective-permute-start | bytes 294920 | tf_op jit(solution)/shard_map/ppermute | solution.py:22
  83.8 9.6 %collective-permute-start.6 = (bf16[2,1,64,384]{3,2,1,0:T(8,128)(2,1)S(1)}, bf16[2,1,64,384]{3,2,1,0:T(8,128)(2,1)S(1)}, u32[]{:S(2)}, u32[]{:S(2)}) collective-permute-start(bf16[2,1,64,384]{3,2,1,0:T(8,128)(2,1)S(1)} %get-tuple-element.84), channel_id=1, source_target_pairs={{0,1},{1,2},{2,3},{3,4},{4,5},{5,6},{6,7},{7,8},{8,9},{9,10},{10,1... | collective-permute-start | bytes 294920 | tf_op jit(solution)/shard_map/ppermute | solution.py:19
  89.2 5.4 %collective-permute-start.7 = (bf16[2,1,64,384]{3,2,1,0:T(8,128)(2,1)S(1)}, bf16[2,1,64,384]{3,2,1,0:T(8,128)(2,1)S(1)}, u32[]{:S(2)}, u32[]{:S(2)}) collective-permute-start(bf16[2,1,64,384]{3,2,1,0:T(8,128)(2,1)S(1)} %get-tuple-element.85), channel_id=1, source_target_pairs={{1,0},{2,1},{3,2},{4,3},{5,4},{6,5},{7,6},{8,7},{9,8},{10,9},{11,1... | collective-permute-start | bytes 294920 | tf_op jit(solution)/shard_map/ppermute | solution.py:22
  102.3 5.0 %copy-start.34 = (f32[768]{0:T(1024)S(1)}, f32[768]{0:T(1024)}, u32[]{:S(2)}) copy-start(f32[768]{0:T(1024)} %get-tuple-element.9) | copy-start | bytes 9220
  102.3 5.0 %copy-start.37 = (f32[384]{0:T(512)S(1)}, f32[384]{0:T(512)}, u32[]{:S(2)}) copy-start(f32[384]{0:T(512)} %get-tuple-element.17) | copy-start | bytes 4612
  102.3 5.0 %copy-start.38 = (f32[384]{0:T(512)S(1)}, f32[384]{0:T(512)}, u32[]{:S(2)}) copy-start(f32[384]{0:T(512)} %get-tuple-element.91) | copy-start | bytes 4612
  102.3 5.6 %copy-start.17 = (bf16[1,1,384,384]{3,2,1,0:T(8,128)(2,1)S(1)}, bf16[1,1,384,384]{3,2,1,0:T(8,128)(2,1)}, u32[]{:S(2)}) copy-start(bf16[1,1,384,384]{3,2,1,0:T(8,128)(2,1)} %get-tuple-element.78) | copy-start | bytes 884740
  114.0 174.5 %copy-start.23 = (bf16[1,256,768]{2,1,0:T(8,128)(2,1)}, bf16[1,256,768]{2,1,0:T(8,128)(2,1)S(1)}, u32[]{:S(2)}) copy-start(bf16[1,256,768]{2,1,0:T(8,128)(2,1)S(1)} %fusion.33) | copy-start | bytes 1179652
  281.9 6.6 %copy-start.14 = (f32[2,384,768]{2,1,0:T(8,128)S(1)}, f32[2,384,768]{2,1,0:T(8,128)}, u32[]{:S(2)}) copy-start(f32[2,384,768]{2,1,0:T(8,128)} %get-tuple-element.130) | copy-start | bytes 7077892
  281.9 8.0 %copy-start.1 = (f32[4,768]{1,0:T(4,128)S(1)}, f32[4,768]{1,0:T(4,128)}, u32[]{:S(2)}) copy-start(f32[4,768]{1,0:T(4,128)} %param.12) | copy-start | bytes 36868
  (27 other events, 46.8 us)
Sparse Core Ops, SparseCore 0:
  102.4 179.4 all-reduce.3
